TPU v7x, 32 devices: a whole 2x2x4 slice. The times are simulated.
32 devices in a mesh: sub: 4 (over y, x), row: 2 (over core), col: 4 (over z).
Axes of the slice: x: 2, y: 2, z: 4, core: 2. Of those that a mesh axis runs over, the one named last changes fastest.
Arguments:
- leaf_rhs: bfloat16 [4, 8, 4, 64, 256], P('sub', 'row', 'col'), may hold values from -6 to 6
- leaf_inverse: bfloat16 [4, 8, 4, 256, 256], P('sub', 'row', 'col'), may hold values from -0.5 to 0.5
- coupling: bfloat16 [4, 16, 8, 4, 256, 256], P('sub', 'row', None, 'col'), may hold values from -0.03125 to 0.03125
- pattern: int32 [4, 16, 8, 4], P('sub', 'row', None, 'col'), may hold values 0 or 1
- top_rhs: bfloat16 [16, 64, 256], replicated, may hold values from -6 to 6
- top_inverse: bfloat16 [16, 256, 256], replicated, may hold values from -0.5 to 0.5
- top_factor: bfloat16 [16, 16, 256, 256], P('row', 'col'), may hold values from -0.09375 to 0.09375
Outputs:
- leaf_solution: bfloat16 [4, 8, 4, 64, 256], P('sub', 'row', 'col')
- top_solution: bfloat16 [16, 64, 256], P('row')
All inputs are finite; a program needn't handle non-finite values. No bound on the sum of `pattern` on one device may be relied on, other than what follows from the above.
Results may differ from a plain program's by a relative error of at most 0.025.
Values may be sent and summed in bfloat16 or wider, within the bound.
A program may use at most 128 MiB of HBM per device.

v0:
```python
import jax
import jax.numpy as jnp
from jax import lax
from jax.sharding import PartitionSpec as P


def spread(block, axis, source):
    block = jnp.where(lax.axis_index(axis) == source, block, jnp.zeros_like(block))
    return lax.psum(block, axis)


def local(leaf_rhs, leaf_inverse, coupling, pattern, top_rhs, top_inverse, top_factor):
    own_rhs = leaf_rhs[0, :, 0]
    own_inverse = jnp.tril(leaf_inverse[0, :, 0])
    coupled = coupling[0, :, :, 0]
    weights = pattern[0, :, :, 0].astype(jnp.bfloat16)
    blocks_row = coupled.shape[0]
    rhs_count = own_rhs.shape[1]
    block_size = own_rhs.shape[2]
    total_top = top_rhs.shape[0]
    leaf_forward = jnp.einsum(
        "inb,idb->ind", own_rhs, own_inverse, preferred_element_type=jnp.float32
    ).astype(jnp.bfloat16)
    block_slice = coupled
    weight_slice = weights
    scaled = (
        lax.all_gather(leaf_forward, "row", axis=0, tiled=True)[None]
        * weight_slice[:, :, None, None]
    )
    partial_value = jnp.einsum(
        "ainb,aieb->ane", scaled, block_slice, preferred_element_type=jnp.float32
    )
    updates = lax.psum(partial_value.astype(jnp.bfloat16), ("sub", "col")).astype(jnp.float32)
    row_start = lax.axis_index("row") * blocks_row
    full_row = lax.all_gather(top_factor, "col", axis=1, tiled=True)
    row_ids = row_start + jnp.arange(blocks_row)

    def forward_step(block_id, carried):
        pending, solved = carried
        local_row = jnp.clip(block_id - row_start, 0, blocks_row - 1)
        owner_row = block_id // blocks_row
        residue = (
            top_rhs[block_id].astype(jnp.float32) - updates[local_row] - pending[local_row]
        ).astype(jnp.bfloat16)
        solved_piece = jnp.dot(
            residue, jnp.tril(top_inverse[block_id]).T, preferred_element_type=jnp.float32
        ).astype(jnp.bfloat16)
        solved_piece = spread(solved_piece, "row", owner_row)
        column = lax.dynamic_index_in_dim(full_row, block_id, 1, keepdims=False)
        below = (row_ids > block_id).astype(jnp.float32)
        pending = pending + below[:, None, None] * jnp.einsum(
            "nb,aeb->ane", solved_piece, column, preferred_element_type=jnp.float32
        )
        solved = lax.dynamic_update_index_in_dim(solved, solved_piece, block_id, 0)
        return (pending, solved)

    start_state = (
        jnp.zeros((blocks_row, rhs_count, block_size), jnp.float32),
        jnp.zeros((total_top, rhs_count, block_size), jnp.bfloat16),
    )
    forward_all = lax.fori_loop(0, total_top, forward_step, start_state)[1]

    def backward_step(iteration, solved):
        block_id = total_top - 1 - iteration
        own_rows = lax.dynamic_slice_in_dim(solved, row_start, blocks_row, 0)
        above = (row_ids > block_id).astype(jnp.bfloat16)
        column = lax.dynamic_index_in_dim(full_row, block_id, 1, keepdims=False)
        term = jnp.einsum(
            "ane,aeb->nb",
            own_rows * above[:, None, None],
            column,
            preferred_element_type=jnp.float32,
        )
        summed = lax.psum(term.astype(jnp.bfloat16), "row").astype(jnp.float32)
        residue = (forward_all[block_id].astype(jnp.float32) - summed).astype(jnp.bfloat16)
        solved_piece = jnp.dot(
            residue, jnp.tril(top_inverse[block_id]), preferred_element_type=jnp.float32
        ).astype(jnp.bfloat16)
        return lax.dynamic_update_index_in_dim(solved, solved_piece, block_id, 0)

    solution = lax.fori_loop(
        0, total_top, backward_step, jnp.zeros((total_top, rhs_count, block_size), jnp.bfloat16)
    )
    own_top = lax.dynamic_slice_in_dim(solution, row_start, blocks_row, 0)
    block_slice = coupled
    weight_slice = weights
    scaled = own_top[:, None] * weight_slice[:, :, None, None]
    back_sums = lax.psum_scatter(
        jnp.einsum(
            "aine,aieb->inb", scaled, block_slice, preferred_element_type=jnp.float32
        ).astype(jnp.bfloat16),
        "row",
        scatter_dimension=0,
        tiled=True,
    ).astype(jnp.float32)
    leaf_residue = (leaf_forward.astype(jnp.float32) - back_sums).astype(jnp.bfloat16)
    leaf_result = jnp.einsum(
        "inb,ibd->ind", leaf_residue, own_inverse, preferred_element_type=jnp.float32
    ).astype(jnp.bfloat16)
    return (leaf_result[None, :, None], own_top)


def solution(mesh):
    placed = (
        P("sub", "row", "col", None, None),
        P("sub", "row", "col", None, None),
        P("sub", "row", None, "col", None, None),
        P("sub", "row", None, "col"),
        P(),
        P(),
        P("row", "col", None, None),
    )
    return jax.shard_map(
        local,
        mesh=mesh,
        in_specs=placed,
        out_specs=(P("sub", "row", "col", None, None), P("row", None, None)),
        check_vma=False,
    )
```

profile of v0, /device:TPU:1, one launch (start us, length us, event | category | flops | bytes accessed | tf_op | source)
XLA Modules:
  0.0 611.1 jit_solution(8503722693803303279)
XLA Ops:
  10.2 2.0 all_gather.7
  12.9 6.7 %fusion.62 = bf16[8,64,256]{2,1,0:T(8,128)(2,1)} fusion(bf16[1,8,8,1,256,256]{5,4,3,2,1,0:T(8,128)(2,1)} %param.13, bf16[8,8]{1,0:T(8,128)(2,1)S(1)} %convert_bitcast_fusion, bf16[8,64,256]{2,1,0:T(8,128)(2,1)S(1)} %all_gather.7), kind=kOutput, calls=%fused_computation.56 | convolution fusion | flops 538050560 | bytes 8913024 | tf_op jit(solution)/shard_map/ainb,aieb->ane/dot_general | solution.py:30
  19.7 4.6 copy.13
  24.4 360.6 %all-reduce.2.cloned.1.call-done = bf16[8,64,256]{2,1,0:T(8,128)(2,1)} async-done(((bf16[8,64,256]{2,1,0:T(8,128)(2,1)}), bf16[8,64,256]{2,1,0:T(8,128)(2,1)}) %all-reduce.2.cloned.1.call-update) | async-done | bytes 262160 | tf_op jit(solution)/shard_map/psum | solution.py:33
  386.0 104.7 %while.37 = (s32[]{:T(128)}, f32[8,64,256]{2,1,0:T(8,128)S(1)}, bf16[16,64,256]{2,1,0:T(8,128)(2,1)S(1)}, bf16[8,16,256,256]{3,2,0,1:T(8,128)(2,1)}, bf16[16,64,...) while((s32[]{:T(128)}, f32[8,64,256]{2,1,0:T(8,128)S(1)}, ...), condition=%wide.region_3.4_spmd.clone.clone.clone, body=%wide.region_1.3_spmd.clone.clone.clone.sunk | while | flops 76136488 | bytes 3639171 | solution.py:61
  387.3 5.7 psum.43
  393.0 1.7 fusion.101
  395.9 3.4 psum.43
  399.4 1.7 fusion.101
  402.2 3.6 psum.43
  405.8 1.7 fusion.101
  408.7 3.4 psum.43
  415.0 3.6 psum.43
  421.5 3.4 psum.43
  427.9 3.6 psum.43
  434.3 3.4 psum.43
  437.8 1.7 fusion.101
  440.7 3.6 psum.43
  444.3 1.7 fusion.101
  447.2 3.4 psum.43
  453.5 3.6 psum.43
  457.1 1.7 fusion.101
  460.0 3.4 psum.43
  466.3 3.6 psum.43
  472.8 3.4 psum.43
  476.2 1.7 fusion.101
  479.1 3.6 psum.43
  485.6 3.4 psum.43
  490.8 98.4 %while.36 = (s32[]{:T(128)}, bf16[16,64,256]{2,1,0:T(8,128)(2,1)S(1)}, bf16[16,64,256]{2,1,0:T(8,128)(2,1)S(1)}, s32[]{:T(128)}, bf16[8,16,256,256]{3,2,0,1:T(8,...) while((s32[]{:T(128)}, ...), condition=%wide.region_6.7_spmd.clone, body=%wide.region_4.6_spmd.clone.sunk | while | flops 75874336 | bytes 1641143 | solution.py:81
  492.4 3.6 psum.42
  498.6 3.4 psum.42
  504.7 3.6 psum.42
  510.9 3.4 psum.42
  517.0 3.6 psum.42
  523.2 3.4 psum.42
  529.3 3.6 psum.42
  535.5 3.4 psum.42
  541.6 3.6 psum.42
  547.8 3.4 psum.42
  553.9 3.6 psum.42
  560.1 3.4 psum.42
  566.2 3.6 psum.42
  572.4 3.4 psum.42
  578.5 3.6 psum.42
  584.7 3.4 psum.42
  589.2 5.8 fusion.57
  595.0 6.8 %reduce-scatter.2.cloned.1.call-done = bf16[4,64,256]{2,1,0:T(8,128)(2,1)} async-done(((bf16[8,64,256]{2,1,0:T(8,128)(2,1)}), bf16[4,64,256]{2,1,0:T(8,128)(2,1)}) %reduce-scatter.2.cloned.1.call-update) | async-done | bytes 131088 | tf_op jit(solution)/shard_map/reduce_scatter | solution.py:88
  601.9 1.8 fusion.68
  (142 shorter events, 79.8 us)
Async XLA Ops:
  8.0 0.9 copy-start
  8.0 377.0 %all-reduce.2.cloned.1.call-start = ((), (), s32[]{:S(2)}) async-start(), calls=%async_computation.2 | async-start | bytes 524288 | tf_op jit(solution)/shard_map/psum | solution.py:33
  19.7 366.3 %all-gather.2.cloned.1.call-start = ((), (), s32[]{:S(2)}) async-start(), calls=%async_computation.1 | async-start | bytes 20971520 | tf_op jit(solution)/shard_map/all_gather | solution.py:35
  24.3 577.6 %reduce-scatter.2.cloned.1.call-start = ((), (), s32[]{:S(2)}) async-start(), calls=%async_computation.3 | async-start | bytes 393216 | tf_op jit(solution)/shard_map/reduce_scatter | solution.py:88
  589.2 5.8 copy-start.1
  589.2 12.7 %copy-start.2 = (bf16[1,4,1,256,256]{4,3,2,1,0:T(8,128)(2,1)S(1)}, bf16[1,4,1,256,256]{4,3,2,1,0:T(8,128)(2,1)}, u32[]{:S(2)}) copy-start(bf16[1,4,1,256,256]{4,3,2,1,0:T(8,128)(2,1)} %param.12) | copy-start | bytes 1572868
Sparse Core Ops, SparseCore 0:
  19.8 365.1 all-reduce.1
  595.2 6.6 reduce-scatter.1
Sparse Core Ops, SparseCore 1:
  24.4 289.3 all-gather.1
where the time goes:
time: 614 us; the launch traced here: 611 us
  waiting for transfers between devices  368 us (60%)
  blocking collectives  116 us (19%)
  matrix products  102 us (17%)
  between operations  15.6 us (3%)
    psum x1, waiting for transfers between devices, local(): lax.psum(partial_value.astype(jnp.bfloat16), ('sub', 'col'))  361 us
    psum x16, blocking collectives, spread(): return lax.psum(block, axis)  58 us
    psum x16, blocking collectives, backward_step(): summed = lax.psum(term.astype(jnp.bfloat16), 'row').astype(jnp.float32)  55.9 us
    dot_general x16, matrix products, forward_step(): jnp.einsum('nb,aeb->ane', solved_piece, column, preferred_element_type=jn...  26.7 us
    dot_general x16, matrix products, backward_step(): jnp.einsum('ane,aeb->nb', own_rows * above[:, None, None], column, prefer...  25.1 us
    dot_general x16, matrix products, forward_step(): jnp.dot(residue, jnp.tril(top_inverse[block_id]).T, preferred_element_typ...  17.5 us
    dot_general x16, matrix products, backward_step(): jnp.dot(residue, jnp.tril(top_inverse[block_id]), preferred_element_type=...  17 us
  transfers between devices with their start and end apart: 3, of which 2 were waited for; matrix products, arithmetic and copies ran while one was open for 1% of the time, Pallas kernels for 0%

commit v1 on v0

v1 whole, which is shorter than its diff:
```python
import functools

import jax
import jax.numpy as jnp
from jax import lax
from jax.experimental import pallas as pl
from jax.experimental.pallas import tpu as pltpu
from jax.sharding import PartitionSpec as P

BF = jnp.bfloat16
F32 = jnp.float32


def dot_nt(a, b):
    return lax.dot_general(a, b, (((1,), (1,)), ((), ())), preferred_element_type=F32)


def dot_nn(a, b):
    return lax.dot_general(a, b, (((1,), (0,)), ((), ())), preferred_element_type=F32)


def lower(block):
    rows = lax.broadcasted_iota(jnp.int32, block.shape, 0)
    cols = lax.broadcasted_iota(jnp.int32, block.shape, 1)
    return jnp.where(rows >= cols, block.astype(F32), 0.0).astype(BF)


def kernel(
    S, R, C,
    pat, rhs_h, linv_h, coup_h, trhs_h, tinv_h, tf_h,
    out, top_h,
    rhs, ginv, gt, coup, y, u, ub, d1, v, d2, tf, ti, tr, W, res, xf,
    fws, fwr, xs, bwr, x, acc, zb, zr,
    ld, cp_sem, y_ss, y_rs, tf_ss, tf_rs, d1_ss, d1_rs, d2_ss, d2_rs,
    fw_ss, fw_rs, bw_ss, bw_rs, x1_ss, x1_rs, x2_ss, x2_rs, z_ss, z_rs,
):
    s, r, c = lax.axis_index("sub"), lax.axis_index("row"), lax.axis_index("col")
    Kr, _, Ni, B, _ = coup.shape
    KT, Kc = tf.shape[:2]
    n = y.shape[2]
    ns = n // S
    Kg = min(Kr, Kc)
    chunks = Kr // Kg
    Q = Kc // Kg
    lead = (c * Kc) // Kr
    is_lead = r == lead
    mine = pl.ds(pl.multiple_of(s * ns, ns), ns)

    def remote(src, dst, ss, rs, dev):
        return pltpu.make_async_remote_copy(
            src_ref=src, dst_ref=dst, send_sem=ss, recv_sem=rs,
            device_id=dev, device_id_type=pl.DeviceIdType.MESH,
        )

    def group_of(j):
        return (r * Kr + j * Kg) // Kc

    loads = [
        pltpu.make_async_copy(linv_h, ginv, ld.at[0]),
        pltpu.make_async_copy(rhs_h, rhs, ld.at[1]),
    ]
    for cp in loads:
        cp.start()

    def coup_copy(a, p):
        rr = lax.rem(r + p, R)
        return pltpu.make_async_copy(coup_h.at[a, rr], coup.at[a, rr], cp_sem.at[a, p])

    for p in range(R):
        for a in range(Kr):
            coup_copy(a, p).start()
    ti_copy = pltpu.make_async_copy(tinv_h.at[pl.ds(c * Kc, Kc)], ti, ld.at[2])
    tr_copy = pltpu.make_async_copy(trhs_h.at[pl.ds(c * Kc, Kc), mine], tr, ld.at[3])
    tf_copy = pltpu.make_async_copy(tf_h, tf.at[pl.ds(r * Kr, Kr)], ld.at[4])

    @pl.when(is_lead)
    def _():
        ti_copy.start()
        tr_copy.start()
        tf_copy.start()

    barrier = pltpu.get_barrier_semaphore()
    for p in range(1, S):
        pl.semaphore_signal(
            barrier, inc=1, device_id=(lax.rem(s + p, S), r, c), device_id_type=pl.DeviceIdType.MESH
        )
    for p in range(R):
        for q in range(C):
            if p == 0 and q == 0:
                continue
            pl.semaphore_signal(
                barrier, inc=1, device_id=(s, lax.rem(r + p, R), lax.rem(c + q, C)),
                device_id_type=pl.DeviceIdType.MESH,
            )

    for cp in loads:
        cp.wait()
    for i in range(Ni):
        g = lower(ginv[i])
        gt[i] = g
        y[r, i] = dot_nt(rhs[i], g).astype(BF)

    pl.semaphore_wait(barrier, S - 1 + R * C - 1)

    def y_send(p):
        return remote(y.at[r], y.at[r], y_ss.at[p], y_rs.at[p], (s, lax.rem(r + p, R), c))

    def y_from(p):
        src = lax.rem(r + R - p, R)
        return remote(y.at[src], y.at[src], y_ss.at[p], y_rs.at[p], (s, src, c))

    for p in range(1, R):
        y_send(p).start()

    tf_send = remote(tf_h, tf.at[pl.ds(r * Kr, Kr)], tf_ss, tf_rs.at[r], (s, lead, c))

    @pl.when(r > lead)
    def _():
        tf_send.start()

    def tf_wait(rr):
        remote(tf_h, tf.at[pl.ds(rr * Kr, Kr)], tf_ss, tf_rs.at[rr], (s, lead, c)).wait_recv()

    def add(a, rr, first):
        total = None if first else u[a]
        for i in range(Ni):
            w = pat[a, rr * Ni + i].astype(F32)
            term = dot_nt(y[rr, i], coup[a, rr, i]) * w
            total = term if total is None else total + term
        return total

    def d1_send(j, p):
        to = lax.rem(s + p, S)
        rows = pl.ds(pl.multiple_of(to * ns, ns), ns)
        blocks = pl.ds(j * Kg, Kg)
        return remote(
            ub.at[blocks, rows], d1.at[p, blocks], d1_ss.at[j, p], d1_rs.at[j, p], (to, r, c)
        )

    for a in range(Kr):
        coup_copy(a, 0).wait()
        u[a] = add(a, r, True)
    for p in range(1, R):
        y_from(R - p).wait_recv()
        for a in range(Kr):
            coup_copy(a, p).wait()
            total = add(a, lax.rem(r + p, R), False)
            if p < R - 1:
                u[a] = total
            else:
                u[a] = total
                ub[a] = total.astype(BF)
                if a % Kg == Kg - 1:
                    for t in range(1, S):
                        d1_send(a // Kg, t).start()

    def d2_send(j):
        g = group_of(j)
        pos = lax.rem(r * Kr + j * Kg, Kc)
        return remote(
            v.at[pl.ds(j * Kg, Kg)], d2.at[c, pl.ds(pos, Kg)], d2_ss.at[j],
            d2_rs.at[pos // Kg, c], (s, (g * Kc) // Kr, g),
        )

    def self_lead(j):
        return jnp.logical_and(is_lead, group_of(j) == c)

    for j in range(chunks):
        for p in range(1, S):
            d1_send(j, p).wait_recv()
        for b in range(Kg):
            a = j * Kg + b
            total = u[a, mine, :]
            for p in range(1, S):
                total = total + d1[p, a].astype(F32)
            v[a] = total.astype(BF)

        @pl.when(self_lead(j))
        def _():
            d2[c, pl.ds(0, Kg)] = v[pl.ds(j * Kg, Kg)]

        @pl.when(jnp.logical_not(self_lead(j)))
        def _():
            d2_send(j).start()

    def blk(k):
        return pl.ds(k * B, B)

    def fw_copy(src_c, dst_c):
        return remote(
            fws.at[dst_c], fwr.at[src_c], fw_ss.at[dst_c], fw_rs.at[src_c],
            (s, (dst_c * Kc) // Kr, dst_c),
        )

    def bw_copy(src_c, dst_c):
        return remote(
            xs, bwr.at[src_c], bw_ss.at[dst_c], bw_rs.at[src_c],
            (s, (dst_c * Kc) // Kr, dst_c),
        )

    def x1_copy(q, to):
        owner = lead + q
        local = c * Kc + q * Kg - owner * Kr
        return remote(
            xs.at[pl.ds(q * Kg, Kg)], x.at[pl.ds(local, Kg), mine], x1_ss.at[q, to],
            x1_rs.at[local // Kg], (s, owner, to),
        )

    @pl.when(is_lead)
    def _():
        ti_copy.wait()
        tf_copy.wait()
        for q in range(1, Q):
            tf_wait(lead + q)
        base = c * Kc
        for k in range(Kc):
            g = lower(ti[k])
            W[blk(k), blk(k)] = g
            for b in range(k):
                t = None
                for m in range(b, k):
                    term = dot_nn(tf[base + k, m], W[blk(m), blk(b)])
                    t = term if t is None else t + term
                W[blk(k), blk(b)] = (-dot_nn(g, t.astype(BF))).astype(BF)
        tr_copy.wait()
        for q in range(Q):
            for o in range(C):
                def take(q=q, o=o):
                    remote(
                        v.at[pl.ds(0, Kg)], d2.at[o, pl.ds(q * Kg, Kg)], d2_ss.at[0],
                        d2_rs.at[q, o], (s, lead + q, o),
                    ).wait_recv()
                if q == 0:
                    pl.when(c != o)(take)
                else:
                    take()
        for k in range(Kc):
            total = tr[k].astype(F32)
            for o in range(C):
                total = total - d2[o, k].astype(F32)
            res[k] = total
        for o in range(C - 1):
            @pl.when(c > o)
            def _(o=o):
                fw_copy(o, c).wait_recv()
                for k in range(Kc):
                    res[k] = res[k] - fwr[o, k].astype(F32)
        rb = [res[k].astype(BF) for k in range(Kc)]
        fb = []
        for k in range(Kc):
            t = dot_nt(rb[k], W[blk(k), blk(k)])
            for b in range(k):
                t = t + dot_nt(rb[b], W[blk(k), blk(b)])
            fb.append(t.astype(BF))
            xf[k] = fb[k]
        for o in range(1, C):
            @pl.when(c < o)
            def _(o=o):
                for rr in range(R):
                    if (rr * Kr) // Kc == o:
                        tf_wait(rr)
                for k in range(Kc):
                    t = None
                    for b in range(Kc):
                        term = dot_nt(xf[b], tf[o * Kc + k, b])
                        t = term if t is None else t + term
                    fws[o, k] = t.astype(BF)
                fw_copy(c, o).start()
        for k in range(Kc):
            res[k] = xf[k].astype(F32)
        for o in range(C - 1, 0, -1):
            @pl.when(c < o)
            def _(o=o):
                bw_copy(o, c).wait_recv()
                for k in range(Kc):
                    t = res[k]
                    for a in range(Kc):
                        t = t - dot_nn(bwr[o, a], tf[o * Kc + a, k])
                    res[k] = t
        wb = [res[k].astype(BF) for k in range(Kc)]
        for k in range(Kc):
            t = dot_nn(wb[k], W[blk(k), blk(k)])
            for a in range(k + 1, Kc):
                t = t + dot_nn(wb[a], W[blk(a), blk(k)])
            xs[k] = t.astype(BF)
        for o in range(C - 2, -1, -1):
            @pl.when(c > o)
            def _(o=o):
                bw_copy(c, o).start()
        local = c * Kc - lead * Kr
        for b in range(Kg):
            x[local + b, mine, :] = xs[b]
        for q in range(Q):
            for o in range(C):
                if q == 0:
                    @pl.when(c != o)
                    def _(q=q, o=o):
                        x1_copy(q, o).start()
                else:
                    x1_copy(q, o).start()

    def x2_copy(j, p):
        place = x.at[pl.ds(j * Kg, Kg), mine]
        return remote(place, place, x2_ss.at[j, p], x2_rs.at[j, p], (lax.rem(s + p, S), r, c))

    def x2_from(j, p):
        src = lax.rem(s + S - p, S)
        place = x.at[pl.ds(j * Kg, Kg), pl.ds(pl.multiple_of(src * ns, ns), ns)]
        return remote(place, place, x2_ss.at[j, p], x2_rs.at[j, p], (src, r, c))

    def z_send(p):
        to = lax.rem(r + p, R)
        return remote(zb.at[p], zr.at[p], z_ss.at[p], z_rs.at[p], (s, to, c))

    for j in range(chunks - 1, -1, -1):
        @pl.when(jnp.logical_not(self_lead(j)))
        def _():
            place = x.at[pl.ds(j * Kg, Kg), mine]
            remote(place, place, x1_ss.at[0, 0], x1_rs.at[j], (s, r, c)).wait_recv()
        for p in range(1, S):
            x2_copy(j, p).start()
        for p in range(1, S):
            x2_from(j, p).wait_recv()
        if j == 0:
            top_copy = pltpu.make_async_copy(x, top_h, ld.at[5])
            top_copy.start()
        for p in [*range(1, R), 0]:
            rr = lax.rem(r + p, R)
            for i in range(Ni):
                t = None if j == chunks - 1 else acc[p, i]
                for b in range(Kg):
                    a = j * Kg + b
                    w = pat[a, rr * Ni + i].astype(F32)
                    term = dot_nn(x[a], coup[a, rr, i]) * w
                    t = term if t is None else t + term
                if j == 0 and p > 0:
                    zb[p, i] = t.astype(BF)
                else:
                    acc[p, i] = t
            if j == 0 and p > 0:
                z_send(p).start()

    for p in range(1, R):
        z_send(p).wait_recv()
    for i in range(Ni):
        t = y[r, i].astype(F32) - acc[0, i]
        for p in range(1, R):
            t = t - zr[p, i].astype(F32)
        out[i] = dot_nn(t.astype(BF), gt[i]).astype(BF)

    top_copy.wait()
    for p in range(1, R):
        y_send(p).wait_send()
        z_send(p).wait_send()

    @pl.when(r > lead)
    def _():
        tf_send.wait_send()

    for j in range(chunks):
        for p in range(1, S):
            d1_send(j, p).wait_send()
            x2_copy(j, p).wait_send()

        @pl.when(jnp.logical_not(self_lead(j)))
        def _():
            d2_send(j).wait_send()

    @pl.when(is_lead)
    def _():
        for o in range(C):
            @pl.when(c < o)
            def _(o=o):
                fw_copy(c, o).wait_send()

            @pl.when(c > o)
            def _(o=o):
                bw_copy(c, o).wait_send()
            for q in range(Q):
                if q == 0:
                    @pl.when(c != o)
                    def _(q=q, o=o):
                        x1_copy(q, o).wait_send()
                else:
                    x1_copy(q, o).wait_send()


def local(sizes, leaf_rhs, leaf_inverse, coupling, pattern, top_rhs, top_inverse, top_factor):
    S, R, C = sizes
    _, Kr, NL, _, B, _ = coupling.shape
    Ni = NL // R
    KT, n, _ = top_rhs.shape
    Kc = top_factor.shape[1]
    ns = n // S
    Kg = min(Kr, Kc)
    chunks, Q = Kr // Kg, Kc // Kg
    V = pltpu.VMEM
    D = pltpu.SemaphoreType.DMA
    any_spec = pl.BlockSpec(memory_space=pl.ANY)
    scratch = [
        V((Ni, n, B), BF), V((Ni, B, B), BF), V((Ni, B, B), BF),
        V((Kr, R, Ni, B, B), BF), V((R, Ni, n, B), BF),
        V((Kr, n, B), F32), V((Kr, n, B), BF), V((S, Kr, ns, B), BF), V((Kr, ns, B), BF),
        V((C, Kc, ns, B), BF), V((KT, Kc, B, B), BF), V((Kc, B, B), BF), V((Kc, ns, B), BF),
        V((Kc * B, Kc * B), BF), V((Kc, ns, B), F32), V((Kc, ns, B), BF),
        V((C, Kc, ns, B), BF), V((C, Kc, ns, B), BF), V((Kc, ns, B), BF), V((C, Kc, ns, B), BF),
        V((Kr, n, B), BF), V((R, Ni, n, B), F32), V((R, Ni, n, B), BF), V((R, Ni, n, B), BF),
        D((6,)), D((Kr, R)), D((R,)), D((R,)), D, D((R,)),
        D((chunks, S)), D((chunks, S)), D((chunks,)), D((Q, C)),
        D((C,)), D((C,)), D((C,)), D((C,)),
        D((Q, C)), D((chunks,)), D((chunks, S)), D((chunks, S)), D((R,)), D((R,)),
    ]
    leaf, top = pl.pallas_call(
        functools.partial(kernel, S, R, C),
        out_shape=(
            jax.ShapeDtypeStruct((Ni, n, B), BF),
            jax.ShapeDtypeStruct((Kr, n, B), BF),
        ),
        in_specs=[pl.BlockSpec(memory_space=pltpu.SMEM)] + [any_spec] * 6,
        out_specs=(pl.BlockSpec(memory_space=pltpu.VMEM), any_spec),
        scratch_shapes=scratch,
        compiler_params=pltpu.CompilerParams(
            collective_id=0, has_side_effects=True, vmem_limit_bytes=56 * 1024 * 1024
        ),
    )(
        pattern.reshape(Kr, NL),
        leaf_rhs.reshape(Ni, n, B),
        leaf_inverse.reshape(Ni, B, B),
        coupling.reshape(Kr, R, Ni, B, B),
        top_rhs,
        top_inverse,
        top_factor,
    )
    return leaf[None, :, None], top


def solution(mesh):
    placed = (
        P("sub", "row", "col", None, None),
        P("sub", "row", "col", None, None),
        P("sub", "row", None, "col", None, None),
        P("sub", "row", None, "col"),
        P(),
        P(),
        P("row", "col", None, None),
    )
    sizes = tuple(mesh.shape[name] for name in ("sub", "row", "col"))
    return jax.shard_map(
        functools.partial(local, sizes),
        mesh=mesh,
        in_specs=placed,
        out_specs=(P("sub", "row", "col", None, None), P("row", None, None)),
        check_vma=False,
    )
```

time: 614 us -> 54 us (0.09)
  waiting for transfers between devices: 368 us -> 0 us
  blocking collectives: 116 us -> 0 us
  matrix products: 102 us -> 0 us
  Pallas kernels: 0 us -> 49.9 us
  between operations: 15.6 us -> 0.64 us
    psum x1 -> x0, waiting for transfers between devices: 361 us -> none  [local(): lax.psum(partial_value.astype(jnp.bfloat16), ('sub', 'col'))]
    psum x32 -> x0, blocking collectives: 114 us -> none  [the longest x16 58 us: spread(): return lax.psum(block, axis)]
    dot_general x68 -> x0, matrix products: 102 us -> none  [the longest x16 26.7 us: forward_step(): jnp.einsum('nb,aeb->ane', solved_piece, column, preferred_element_type=jn...]
    pallas_call x0 -> x1, Pallas kernels: none -> 49.9 us  [local(): pl.pallas_call(functools.partial(kernel, S, R, C), out_shape=(jax.ShapeDt...]
    reduce_scatter x1 -> x0, waiting for transfers between devices: 6.84 us -> none  [local(): lax.psum_scatter(jnp.einsum('aine,aieb->inb', scaled, block_slice, prefer...]
  transfers between devices with their start and end apart: 3 -> 0, of which waited for: 2 -> 0; matrix products, arithmetic and copies ran while one was open for 1% -> 0% of each run, Pallas kernels for 0% -> 0%
where the time goes in v1:
time: 54 us; the launch traced here: 53.8 us
  Pallas kernels  49.9 us (92%)
  local copies, waits for them, and re-layouts  3.24 us (6%)
  between operations  0.64 us (1%)
    pallas_call x1, Pallas kernels, local(): pl.pallas_call(functools.partial(kernel, S, R, C), out_shape=(jax.ShapeDt...  49.9 us
    unnamed x2, local copies, waits for them, and re-layouts  3.24 us

profile of v1, /device:TPU:1, one launch (start us, length us, event | category | flops | bytes accessed | tf_op | source)
XLA Modules:
  0.0 53.8 jit_solution(11248911025269475355)
XLA Ops:
  0.6 49.9 %shard_map.86 = (bf16[4,64,256]{2,1,0:T(8,128)(2,1)}, bf16[8,64,256]{2,1,0:T(8,128)(2,1)}) custom-call(s32[8,8]{1,0:T(8,128)} %bitcast.11, bf16[4,64,256]{2,1,0:T(8,128)(2,1)} %bitcast.9, bf16[4,256,256]{2,1,0:T(8,128)(2,1)} %bitcast.8, bf16[8,2,4,256,256]{4,3,2,1,0:T(8,128)(2,1)} %bitcast.7, bf16[16,64,256]{2,1,0:T(8,128)(2,1)} %trhs_h.1, ...), custom_call_target="tpu_custom_call" | custom-call | tf_op jit(solution)/shard_map/pallas_call | solution.py:413
  50.5 1.6 %copy.12 = bf16[1,4,1,64,256]{4,3,2,1,0:T(8,128)(2,1)} copy(bf16[1,4,1,64,256]{4,3,2,1,0:T(8,128)(2,1)} %bitcast.10) | data formatting | bytes 262144
  52.1 1.7 %copy.13 = bf16[8,64,256]{2,1,0:T(8,128)(2,1)} copy(bf16[8,64,256]{2,1,0:T(8,128)(2,1)} %get-tuple-element.11) | data formatting | bytes 524288

commit v2 on v1

--- a/solution.py
+++ b/solution.py
@@ -28,7 +28,7 @@
 def kernel(
     S, R, C,
     pat, rhs_h, linv_h, coup_h, trhs_h, tinv_h, tf_h,
-    out, top_h,
+    out, top,
     rhs, ginv, gt, coup, y, u, ub, d1, v, d2, tf, ti, tr, W, res, xf,
     fws, fwr, xs, bwr, x, acc, zb, zr,
     ld, cp_sem, y_ss, y_rs, tf_ss, tf_rs, d1_ss, d1_rs, d2_ss, d2_rs,
@@ -165,6 +165,28 @@
     def self_lead(j):
         return jnp.logical_and(is_lead, group_of(j) == c)
 
+    def blk(k):
+        return pl.ds(k * B, B)
+
+    def w_row(k):
+        g = lower(ti[k])
+        W[blk(k), blk(k)] = g
+        for b in range(k):
+            t = None
+            for m in range(b, k):
+                term = dot_nn(tf[c * Kc + k, m], W[blk(m), blk(b)])
+                t = term if t is None else t + term
+            W[blk(k), blk(b)] = (-dot_nn(g, t.astype(BF))).astype(BF)
+
+    @pl.when(is_lead)
+    def _():
+        ti_copy.wait()
+        tf_copy.wait()
+        for q in range(1, Q):
+            tf_wait(lead + q)
+        for k in range(Kc - 1):
+            w_row(k)
+
     for j in range(chunks):
         for p in range(1, S):
             d1_send(j, p).wait_recv()
@@ -183,9 +205,6 @@
         def _():
             d2_send(j).start()
 
-    def blk(k):
-        return pl.ds(k * B, B)
-
     def fw_copy(src_c, dst_c):
         return remote(
             fws.at[dst_c], fwr.at[src_c], fw_ss.at[dst_c], fw_rs.at[src_c],
@@ -206,22 +225,17 @@
             x1_rs.at[local // Kg], (s, owner, to),
         )
 
+    def x2_copy(j, p):
+        place = x.at[pl.ds(j * Kg, Kg), mine]
+        return remote(place, place, x2_ss.at[j, p], x2_rs.at[j, p], (lax.rem(s + p, S), r, c))
+
+    def x1_wait(j):
+        place = x.at[pl.ds(j * Kg, Kg), mine]
+        remote(place, place, x1_ss.at[0, 0], x1_rs.at[j], (s, r, c)).wait_recv()
+
     @pl.when(is_lead)
     def _():
-        ti_copy.wait()
-        tf_copy.wait()
-        for q in range(1, Q):
-            tf_wait(lead + q)
-        base = c * Kc
-        for k in range(Kc):
-            g = lower(ti[k])
-            W[blk(k), blk(k)] = g
-            for b in range(k):
-                t = None
-                for m in range(b, k):
-                    term = dot_nn(tf[base + k, m], W[blk(m), blk(b)])
-                    t = term if t is None else t + term
-                W[blk(k), blk(b)] = (-dot_nn(g, t.astype(BF))).astype(BF)
+        w_row(Kc - 1)
         tr_copy.wait()
         for q in range(Q):
             for o in range(C):
@@ -277,6 +291,13 @@
                     for a in range(Kc):
                         t = t - dot_nn(bwr[o, a], tf[o * Kc + a, k])
                     res[k] = t
+
+                @pl.when((o * Kc) // Kr == lead)
+                def _():
+                    j = (o * Kc - lead * Kr) // Kg
+                    x1_wait(j)
+                    for p in range(1, S):
+                        x2_copy(j, p).start()
         wb = [res[k].astype(BF) for k in range(Kc)]
         for k in range(Kc):
             t = dot_nn(wb[k], W[blk(k), blk(k)])
@@ -290,6 +311,8 @@
         local = c * Kc - lead * Kr
         for b in range(Kg):
             x[local + b, mine, :] = xs[b]
+        for p in range(1, S):
+            x2_copy(local // Kg, p).start()
         for q in range(Q):
             for o in range(C):
                 if q == 0:
@@ -299,10 +322,6 @@
                 else:
                     x1_copy(q, o).start()
 
-    def x2_copy(j, p):
-        place = x.at[pl.ds(j * Kg, Kg), mine]
-        return remote(place, place, x2_ss.at[j, p], x2_rs.at[j, p], (lax.rem(s + p, S), r, c))
-
     def x2_from(j, p):
         src = lax.rem(s + S - p, S)
         place = x.at[pl.ds(j * Kg, Kg), pl.ds(pl.multiple_of(src * ns, ns), ns)]
@@ -313,17 +332,15 @@
         return remote(zb.at[p], zr.at[p], z_ss.at[p], z_rs.at[p], (s, to, c))
 
     for j in range(chunks - 1, -1, -1):
-        @pl.when(jnp.logical_not(self_lead(j)))
+        @pl.when(jnp.logical_not(jnp.logical_and(is_lead, group_of(j) >= c)))
         def _():
-            place = x.at[pl.ds(j * Kg, Kg), mine]
-            remote(place, place, x1_ss.at[0, 0], x1_rs.at[j], (s, r, c)).wait_recv()
-        for p in range(1, S):
-            x2_copy(j, p).start()
+            x1_wait(j)
+            for p in range(1, S):
+                x2_copy(j, p).start()
         for p in range(1, S):
             x2_from(j, p).wait_recv()
         if j == 0:
-            top_copy = pltpu.make_async_copy(x, top_h, ld.at[5])
-            top_copy.start()
+            top[...] = x[...]
         for p in [*range(1, R), 0]:
             rr = lax.rem(r + p, R)
             for i in range(Ni):
@@ -348,7 +365,6 @@
             t = t - zr[p, i].astype(F32)
         out[i] = dot_nn(t.astype(BF), gt[i]).astype(BF)
 
-    top_copy.wait()
     for p in range(1, R):
         y_send(p).wait_send()
         z_send(p).wait_send()
@@ -383,6 +399,17 @@
                         x1_copy(q, o).wait_send()
                 else:
                     x1_copy(q, o).wait_send()
+
+
+def write(leaf, top, leaf_h, top_h, sem):
+    copies = [
+        pltpu.make_async_copy(top, top_h, sem.at[0]),
+        pltpu.make_async_copy(leaf, leaf_h, sem.at[1]),
+    ]
+    for cp in copies:
+        cp.start()
+    for cp in copies:
+        cp.wait()
 
 
 def local(sizes, leaf_rhs, leaf_inverse, coupling, pattern, top_rhs, top_inverse, top_factor):
@@ -405,7 +432,7 @@
         V((Kc * B, Kc * B), BF), V((Kc, ns, B), F32), V((Kc, ns, B), BF),
         V((C, Kc, ns, B), BF), V((C, Kc, ns, B), BF), V((Kc, ns, B), BF), V((C, Kc, ns, B), BF),
         V((Kr, n, B), BF), V((R, Ni, n, B), F32), V((R, Ni, n, B), BF), V((R, Ni, n, B), BF),
-        D((6,)), D((Kr, R)), D((R,)), D((R,)), D, D((R,)),
+        D((5,)), D((Kr, R)), D((R,)), D((R,)), D, D((R,)),
         D((chunks, S)), D((chunks, S)), D((chunks,)), D((Q, C)),
         D((C,)), D((C,)), D((C,)), D((C,)),
         D((Q, C)), D((chunks,)), D((chunks, S)), D((chunks, S)), D((R,)), D((R,)),
@@ -413,11 +440,11 @@
     leaf, top = pl.pallas_call(
         functools.partial(kernel, S, R, C),
         out_shape=(
-            jax.ShapeDtypeStruct((Ni, n, B), BF),
-            jax.ShapeDtypeStruct((Kr, n, B), BF),
+            pltpu.VMEM((Ni, n, B), BF),
+            pltpu.VMEM((Kr, n, B), BF),
         ),
         in_specs=[pl.BlockSpec(memory_space=pltpu.SMEM)] + [any_spec] * 6,
-        out_specs=(pl.BlockSpec(memory_space=pltpu.VMEM), any_spec),
+        out_specs=(pl.BlockSpec(memory_space=pltpu.VMEM),) * 2,
         scratch_shapes=scratch,
         compiler_params=pltpu.CompilerParams(
             collective_id=0, has_side_effects=True, vmem_limit_bytes=56 * 1024 * 1024
@@ -431,6 +458,17 @@
         top_inverse,
         top_factor,
     )
+    leaf, top = pl.pallas_call(
+        write,
+        out_shape=(
+            jax.ShapeDtypeStruct((Ni, n, B), BF),
+            jax.ShapeDtypeStruct((Kr, n, B), BF),
+        ),
+        in_specs=[pl.BlockSpec(memory_space=pltpu.VMEM)] * 2,
+        out_specs=(any_spec, any_spec),
+        scratch_shapes=[D((2,))],
+        cost_estimate=pl.CostEstimate(flops=0, bytes_accessed=4 * (Ni + Kr) * n * B, transcendentals=0),
+    )(leaf, top)
     return leaf[None, :, None], top
 
 

time: 54 us -> 52.4 us (0.970)
  the two profiles are of different devices: /device:TPU:1 before, /device:TPU:25 now
where the time goes in v2:
time: 52.4 us; the launch traced here: 52.2 us
  Pallas kernels  50.3 us (96%)
  local copies, waits for them, and re-layouts  1.34 us (3%)
  between operations  0.65 us (1%)
    pallas_call x1, Pallas kernels, local(): pl.pallas_call(functools.partial(kernel, S, R, C), out_shape=(pltpu.VMEM(...  48.5 us
    pallas_call x1, Pallas kernels, local(): pl.pallas_call(write, out_shape=(jax.ShapeDtypeStruct((Ni, n, B), BF), ja...  1.78 us
    unnamed x4, local copies, waits for them, and re-layouts  1.34 us

profile of v2, /device:TPU:25, one launch (start us, length us, event | category | flops | bytes accessed | tf_op | source)
XLA Modules:
  0.0 52.2 jit_solution(16766611049826544784)
XLA Ops:
  0.6 48.5 %shard_map.86 = (bf16[4,64,256]{2,1,0:T(8,128)(2,1)S(1)}, bf16[8,64,256]{2,1,0:T(8,128)(2,1)S(1)}) custom-call(s32[8,8]{1,0:T(8,128)} %bitcast.10, bf16[4,64,256]{2,1,0:T(8,128)(2,1)} %bitcast.9, bf16[4,256,256]{2,1,0:T(8,128)(2,1)} %bitcast.8, bf16[8,2,4,256,256]{4,3,2,1,0:T(8,128)(2,1)} %bitcast.7, bf16[16,64,256]{2,1,0:T(8,128)(2,1)} %trhs_h.1, ...), custom_call_target="tpu_custom_call" | custom-call | tf_op jit(solution)/shard_map/pallas_call | solution.py:440
  49.1 0.0 copy-start
  49.1 0.7 %copy-done = bf16[8,64,256]{2,1,0:T(8,128)(2,1)} copy-done((bf16[8,64,256]{2,1,0:T(8,128)(2,1)}, bf16[8,64,256]{2,1,0:T(8,128)(2,1)S(1)}, u32[]{:S(2)}) %copy-start) | copy-done | bytes 262168
  49.8 0.0 copy-start.1
  49.8 0.7 %copy-done.1 = bf16[4,64,256]{2,1,0:T(8,128)(2,1)} copy-done((bf16[4,64,256]{2,1,0:T(8,128)(2,1)}, bf16[4,64,256]{2,1,0:T(8,128)(2,1)S(1)}, u32[]{:S(2)}) %copy-start.1) | copy-done | bytes 131096
  50.5 1.8 %shard_map.87 = (bf16[4,64,256]{2,1,0:T(8,128)(2,1)}, bf16[8,64,256]{2,1,0:T(8,128)(2,1)}) custom-call(bf16[4,64,256]{2,1,0:T(8,128)(2,1)} %copy-done.1, bf16[8,64,256]{2,1,0:T(8,128)(2,1)} %copy-done), custom_call_target="tpu_custom_call" | custom-call | bytes 786432 | tf_op jit(solution)/shard_map/pallas_call | solution.py:461
Async XLA Ops:
  49.1 0.7 %copy-start = (bf16[8,64,256]{2,1,0:T(8,128)(2,1)}, bf16[8,64,256]{2,1,0:T(8,128)(2,1)S(1)}, u32[]{:S(2)}) copy-start(bf16[8,64,256]{2,1,0:T(8,128)(2,1)S(1)} %get-tuple-element.7.top) | copy-start | bytes 786436
  49.8 0.7 %copy-start.1 = (bf16[4,64,256]{2,1,0:T(8,128)(2,1)}, bf16[4,64,256]{2,1,0:T(8,128)(2,1)S(1)}, u32[]{:S(2)}) copy-start(bf16[4,64,256]{2,1,0:T(8,128)(2,1)S(1)} %get-tuple-element.6.leaf) | copy-start | bytes 393220

commit v3 on v1

--- a/solution.py
+++ b/solution.py
@@ -28,11 +28,11 @@
 def kernel(
     S, R, C,
     pat, rhs_h, linv_h, coup_h, trhs_h, tinv_h, tf_h,
-    out, top_h,
+    out, top,
     rhs, ginv, gt, coup, y, u, ub, d1, v, d2, tf, ti, tr, W, res, xf,
-    fws, fwr, xs, bwr, x, acc, zb, zr,
+    fws, fwr, xs, x, acc, cx, pf, px,
     ld, cp_sem, y_ss, y_rs, tf_ss, tf_rs, d1_ss, d1_rs, d2_ss, d2_rs,
-    fw_ss, fw_rs, bw_ss, bw_rs, x1_ss, x1_rs, x2_ss, x2_rs, z_ss, z_rs,
+    fw_ss, fw_rs, x1_ss, x1_rs, x2_ss, x2_rs, cx_ss, cx_rs, px_ss, px_rs,
 ):
     s, r, c = lax.axis_index("sub"), lax.axis_index("row"), lax.axis_index("col")
     Kr, _, Ni, B, _ = coup.shape
@@ -66,9 +66,10 @@
         rr = lax.rem(r + p, R)
         return pltpu.make_async_copy(coup_h.at[a, rr], coup.at[a, rr], cp_sem.at[a, p])
 
-    for p in range(R):
-        for a in range(Kr):
-            coup_copy(a, p).start()
+    for j in range(chunks):
+        for p in range(R):
+            for a in range(j * Kg, (j + 1) * Kg):
+                coup_copy(a, p).start()
     ti_copy = pltpu.make_async_copy(tinv_h.at[pl.ds(c * Kc, Kc)], ti, ld.at[2])
     tr_copy = pltpu.make_async_copy(trhs_h.at[pl.ds(c * Kc, Kc), mine], tr, ld.at[3])
     tf_copy = pltpu.make_async_copy(tf_h, tf.at[pl.ds(r * Kr, Kr)], ld.at[4])
@@ -137,22 +138,20 @@
             ub.at[blocks, rows], d1.at[p, blocks], d1_ss.at[j, p], d1_rs.at[j, p], (to, r, c)
         )
 
-    for a in range(Kr):
-        coup_copy(a, 0).wait()
-        u[a] = add(a, r, True)
-    for p in range(1, R):
-        y_from(R - p).wait_recv()
-        for a in range(Kr):
-            coup_copy(a, p).wait()
-            total = add(a, lax.rem(r + p, R), False)
-            if p < R - 1:
+    for j in range(chunks):
+        blocks = range(j * Kg, (j + 1) * Kg)
+        for p in range(R):
+            if j == 0 and p > 0:
+                y_from(R - p).wait_recv()
+            for a in blocks:
+                coup_copy(a, p).wait()
+            for a in blocks:
+                total = add(a, lax.rem(r + p, R), p == 0)
                 u[a] = total
-            else:
-                u[a] = total
-                ub[a] = total.astype(BF)
-                if a % Kg == Kg - 1:
-                    for t in range(1, S):
-                        d1_send(a // Kg, t).start()
+                if p == R - 1:
+                    ub[a] = total.astype(BF)
+        for t in range(1, S):
+            d1_send(j, t).start()
 
     def d2_send(j):
         g = group_of(j)
@@ -164,6 +163,19 @@
 
     def self_lead(j):
         return jnp.logical_and(is_lead, group_of(j) == c)
+
+    def blk(k):
+        return pl.ds(k * B, B)
+
+    def w_row(k):
+        g = lower(ti[k])
+        W[blk(k), blk(k)] = g
+        for b in range(k):
+            t = None
+            for m in range(b, k):
+                term = dot_nn(tf[c * Kc + k, m], W[blk(m), blk(b)])
+                t = term if t is None else t + term
+            W[blk(k), blk(b)] = (-dot_nn(g, t.astype(BF))).astype(BF)
 
     for j in range(chunks):
         for p in range(1, S):
@@ -183,8 +195,25 @@
         def _():
             d2_send(j).start()
 
-    def blk(k):
-        return pl.ds(k * B, B)
+    def cx_send(p):
+        to = lax.rem(r + p, R)
+        return remote(coup_h.at[:, to], cx.at[r], cx_ss.at[p], cx_rs.at[r], (s, to, c))
+
+    def px_send(p):
+        to = lax.rem(r + p, R)
+        return remote(pf.at[to], px.at[r], px_ss.at[p], px_rs.at[r], (s, to, c))
+
+    cx_own = pltpu.make_async_copy(coup_h.at[:, r], cx.at[r], ld.at[5])
+    cx_own.start()
+    for p in range(1, R):
+        cx_send(p).start()
+    for rr in range(R):
+        for a in range(Kr):
+            for i in range(Ni):
+                pf[rr, a, i] = jnp.full((8, B), pat[a, rr * Ni + i].astype(F32))
+    px[r] = pf[r]
+    for p in range(1, R):
+        px_send(p).start()
 
     def fw_copy(src_c, dst_c):
         return remote(
@@ -192,19 +221,21 @@
             (s, (dst_c * Kc) // Kr, dst_c),
         )
 
-    def bw_copy(src_c, dst_c):
+    def x1_copy(rr, o):
         return remote(
-            xs, bwr.at[src_c], bw_ss.at[dst_c], bw_rs.at[src_c],
-            (s, (dst_c * Kc) // Kr, dst_c),
-        )
-
-    def x1_copy(q, to):
-        owner = lead + q
-        local = c * Kc + q * Kg - owner * Kr
-        return remote(
-            xs.at[pl.ds(q * Kg, Kg)], x.at[pl.ds(local, Kg), mine], x1_ss.at[q, to],
-            x1_rs.at[local // Kg], (s, owner, to),
-        )
+            xs, x.at[pl.ds(c * Kc, Kc), mine], x1_ss.at[rr, o], x1_rs.at[c], (s, rr, o)
+        )
+
+    def lead_of(o):
+        return (o * Kc) // Kr
+
+    def x2_copy(g, p):
+        place = x.at[pl.ds(g * Kc, Kc), mine]
+        return remote(place, place, x2_ss.at[g, p], x2_rs.at[g, p], (lax.rem(s + p, S), r, c))
+
+    def x1_wait(g):
+        place = x.at[pl.ds(g * Kc, Kc), mine]
+        remote(place, place, x1_ss.at[0, 0], x1_rs.at[g], (s, r, c)).wait_recv()
 
     @pl.when(is_lead)
     def _():
@@ -212,16 +243,8 @@
         tf_copy.wait()
         for q in range(1, Q):
             tf_wait(lead + q)
-        base = c * Kc
         for k in range(Kc):
-            g = lower(ti[k])
-            W[blk(k), blk(k)] = g
-            for b in range(k):
-                t = None
-                for m in range(b, k):
-                    term = dot_nn(tf[base + k, m], W[blk(m), blk(b)])
-                    t = term if t is None else t + term
-                W[blk(k), blk(b)] = (-dot_nn(g, t.astype(BF))).astype(BF)
+            w_row(k)
         tr_copy.wait()
         for q in range(Q):
             for o in range(C):
@@ -271,12 +294,14 @@
         for o in range(C - 1, 0, -1):
             @pl.when(c < o)
             def _(o=o):
-                bw_copy(o, c).wait_recv()
+                x1_wait(o)
                 for k in range(Kc):
                     t = res[k]
                     for a in range(Kc):
-                        t = t - dot_nn(bwr[o, a], tf[o * Kc + a, k])
+                        t = t - dot_nn(x[o * Kc + a, mine, :], tf[o * Kc + a, k])
                     res[k] = t
+                for p in range(1, S):
+                    x2_copy(o, p).start()
         wb = [res[k].astype(BF) for k in range(Kc)]
         for k in range(Kc):
             t = dot_nn(wb[k], W[blk(k), blk(k)])
@@ -286,72 +311,55 @@
         for o in range(C - 2, -1, -1):
             @pl.when(c > o)
             def _(o=o):
-                bw_copy(c, o).start()
-        local = c * Kc - lead * Kr
-        for b in range(Kg):
-            x[local + b, mine, :] = xs[b]
-        for q in range(Q):
+                x1_copy(lead_of(o), o).start()
+        for b in range(Kc):
+            x[c * Kc + b, mine, :] = xs[b]
+        for p in range(1, S):
+            x2_copy(c, p).start()
+        for rr in range(R):
             for o in range(C):
-                if q == 0:
-                    @pl.when(c != o)
-                    def _(q=q, o=o):
-                        x1_copy(q, o).start()
+                if rr != lead_of(o):
+                    x1_copy(rr, o).start()
                 else:
-                    x1_copy(q, o).start()
-
-    def x2_copy(j, p):
-        place = x.at[pl.ds(j * Kg, Kg), mine]
-        return remote(place, place, x2_ss.at[j, p], x2_rs.at[j, p], (lax.rem(s + p, S), r, c))
-
-    def x2_from(j, p):
+                    @pl.when(c < o)
+                    def _(rr=rr, o=o):
+                        x1_copy(rr, o).start()
+
+    def x2_from(g, p):
         src = lax.rem(s + S - p, S)
-        place = x.at[pl.ds(j * Kg, Kg), pl.ds(pl.multiple_of(src * ns, ns), ns)]
-        return remote(place, place, x2_ss.at[j, p], x2_rs.at[j, p], (src, r, c))
-
-    def z_send(p):
-        to = lax.rem(r + p, R)
-        return remote(zb.at[p], zr.at[p], z_ss.at[p], z_rs.at[p], (s, to, c))
-
-    for j in range(chunks - 1, -1, -1):
-        @pl.when(jnp.logical_not(self_lead(j)))
+        place = x.at[pl.ds(g * Kc, Kc), pl.ds(pl.multiple_of(src * ns, ns), ns)]
+        return remote(place, place, x2_ss.at[g, p], x2_rs.at[g, p], (src, r, c))
+
+    cx_own.wait()
+    for p in range(1, R):
+        src = lax.rem(r + p, R)
+        remote(coup_h.at[:, r], cx.at[src], cx_ss.at[p], cx_rs.at[src], (s, src, c)).wait_recv()
+        remote(pf.at[r], px.at[src], px_ss.at[p], px_rs.at[src], (s, src, c)).wait_recv()
+
+    for g in range(C - 1, -1, -1):
+        @pl.when(jnp.logical_not(jnp.logical_and(is_lead, c <= g)))
         def _():
-            place = x.at[pl.ds(j * Kg, Kg), mine]
-            remote(place, place, x1_ss.at[0, 0], x1_rs.at[j], (s, r, c)).wait_recv()
+            x1_wait(g)
+            for p in range(1, S):
+                x2_copy(g, p).start()
         for p in range(1, S):
-            x2_copy(j, p).start()
-        for p in range(1, S):
-            x2_from(j, p).wait_recv()
-        if j == 0:
-            top_copy = pltpu.make_async_copy(x, top_h, ld.at[5])
-            top_copy.start()
-        for p in [*range(1, R), 0]:
-            rr = lax.rem(r + p, R)
-            for i in range(Ni):
-                t = None if j == chunks - 1 else acc[p, i]
-                for b in range(Kg):
-                    a = j * Kg + b
-                    w = pat[a, rr * Ni + i].astype(F32)
-                    term = dot_nn(x[a], coup[a, rr, i]) * w
-                    t = term if t is None else t + term
-                if j == 0 and p > 0:
-                    zb[p, i] = t.astype(BF)
-                else:
-                    acc[p, i] = t
-            if j == 0 and p > 0:
-                z_send(p).start()
-
-    for p in range(1, R):
-        z_send(p).wait_recv()
-    for i in range(Ni):
-        t = y[r, i].astype(F32) - acc[0, i]
-        for p in range(1, R):
-            t = t - zr[p, i].astype(F32)
-        out[i] = dot_nn(t.astype(BF), gt[i]).astype(BF)
-
-    top_copy.wait()
+            x2_from(g, p).wait_recv()
+        for i in range(Ni):
+            t = y[r, i].astype(F32) if g == C - 1 else acc[i]
+            for b in range(Kc):
+                a = g * Kc + b
+                owner, at = a // Kr, a % Kr
+                t = t - dot_nn(x[a], cx[owner, at, i]) * px[owner, at, i, 0:1, :]
+            if g > 0:
+                acc[i] = t
+            else:
+                out[i] = dot_nn(t.astype(BF), gt[i]).astype(BF)
+    top[...] = x[pl.ds(r * Kr, Kr)]
+
     for p in range(1, R):
         y_send(p).wait_send()
-        z_send(p).wait_send()
+        cx_send(p).wait_send()
+        px_send(p).wait_send()
 
     @pl.when(r > lead)
     def _():
@@ -360,11 +368,14 @@
     for j in range(chunks):
         for p in range(1, S):
             d1_send(j, p).wait_send()
-            x2_copy(j, p).wait_send()
 
         @pl.when(jnp.logical_not(self_lead(j)))
         def _():
             d2_send(j).wait_send()
+
+    for g in range(C):
+        for p in range(1, S):
+            x2_copy(g, p).wait_send()
 
     @pl.when(is_lead)
     def _():
@@ -373,16 +384,13 @@
             def _(o=o):
                 fw_copy(c, o).wait_send()
 
-            @pl.when(c > o)
-            def _(o=o):
-                bw_copy(c, o).wait_send()
-            for q in range(Q):
-                if q == 0:
+            for rr in range(R):
+                if rr != lead_of(o):
+                    x1_copy(rr, o).wait_send()
+                else:
                     @pl.when(c != o)
-                    def _(q=q, o=o):
-                        x1_copy(q, o).wait_send()
-                else:
-                    x1_copy(q, o).wait_send()
+                    def _(rr=rr, o=o):
+                        x1_copy(rr, o).wait_send()
 
 
 def local(sizes, leaf_rhs, leaf_inverse, coupling, pattern, top_rhs, top_inverse, top_factor):
@@ -403,21 +411,22 @@
         V((Kr, n, B), F32), V((Kr, n, B), BF), V((S, Kr, ns, B), BF), V((Kr, ns, B), BF),
         V((C, Kc, ns, B), BF), V((KT, Kc, B, B), BF), V((Kc, B, B), BF), V((Kc, ns, B), BF),
         V((Kc * B, Kc * B), BF), V((Kc, ns, B), F32), V((Kc, ns, B), BF),
-        V((C, Kc, ns, B), BF), V((C, Kc, ns, B), BF), V((Kc, ns, B), BF), V((C, Kc, ns, B), BF),
-        V((Kr, n, B), BF), V((R, Ni, n, B), F32), V((R, Ni, n, B), BF), V((R, Ni, n, B), BF),
+        V((C, Kc, ns, B), BF), V((C, Kc, ns, B), BF), V((Kc, ns, B), BF),
+        V((KT, n, B), BF), V((Ni, n, B), F32), V((R, Kr, Ni, B, B), BF),
+        V((R, Kr, Ni, 8, B), F32), V((R, Kr, Ni, 8, B), F32),
         D((6,)), D((Kr, R)), D((R,)), D((R,)), D, D((R,)),
         D((chunks, S)), D((chunks, S)), D((chunks,)), D((Q, C)),
-        D((C,)), D((C,)), D((C,)), D((C,)),
-        D((Q, C)), D((chunks,)), D((chunks, S)), D((chunks, S)), D((R,)), D((R,)),
+        D((C,)), D((C,)),
+        D((R, C)), D((C,)), D((C, S)), D((C, S)), D((R,)), D((R,)), D((R,)), D((R,)),
     ]
     leaf, top = pl.pallas_call(
         functools.partial(kernel, S, R, C),
         out_shape=(
-            jax.ShapeDtypeStruct((Ni, n, B), BF),
-            jax.ShapeDtypeStruct((Kr, n, B), BF),
+            pltpu.VMEM((Ni, n, B), BF),
+            pltpu.VMEM((Kr, n, B), BF),
         ),
         in_specs=[pl.BlockSpec(memory_space=pltpu.SMEM)] + [any_spec] * 6,
-        out_specs=(pl.BlockSpec(memory_space=pltpu.VMEM), any_spec),
+        out_specs=(pl.BlockSpec(memory_space=pltpu.VMEM),) * 2,
         scratch_shapes=scratch,
         compiler_params=pltpu.CompilerParams(
             collective_id=0, has_side_effects=True, vmem_limit_bytes=56 * 1024 * 1024

time: 54 us -> 48.3 us (0.89)
  Pallas kernels: 49.9 us -> 46.1 us
  local copies, waits for them, and re-layouts: 3.24 us -> 1.36 us
    pallas_call x1, Pallas kernels: 49.9 us -> 46.1 us  [local(): pl.pallas_call(functools.partial(kernel, S, R, C), out_shape=(pltpu.VMEM(...]
    unnamed x2, local copies, waits for them, and re-layouts: 3.24 us -> 1.36 us
where the time goes in v3:
time: 48.3 us; the launch traced here: 48.1 us
  Pallas kernels  46.1 us (95%)
  local copies, waits for them, and re-layouts  1.36 us (3%)
  between operations  0.64 us (1%)
    pallas_call x1, Pallas kernels, local(): pl.pallas_call(functools.partial(kernel, S, R, C), out_shape=(pltpu.VMEM(...  46.1 us
    unnamed x2, local copies, waits for them, and re-layouts  1.36 us

profile of v3, /device:TPU:1, one launch (start us, length us, event | category | flops | bytes accessed | tf_op | source)
XLA Modules:
  0.0 48.1 jit_solution(111956323658096352)
XLA Ops:
  0.6 46.1 %shard_map.86 = (bf16[4,64,256]{2,1,0:T(8,128)(2,1)S(1)}, bf16[8,64,256]{2,1,0:T(8,128)(2,1)S(1)}) custom-call(s32[8,8]{1,0:T(8,128)} %bitcast.11, bf16[4,64,256]{2,1,0:T(8,128)(2,1)} %bitcast.10, bf16[4,256,256]{2,1,0:T(8,128)(2,1)} %bitcast.9, bf16[8,2,4,256,256]{4,3,2,1,0:T(8,128)(2,1)} %bitcast.8, bf16[16,64,256]{2,1,0:T(8,128)(2,1)} %trhs_h.1, ...), custom_call_target="tpu_custom_call" | custom-call | tf_op jit(solution)/shard_map/pallas_call | solution.py:422
  46.7 0.7 %copy.12 = bf16[1,4,1,64,256]{4,3,2,1,0:T(8,128)(2,1)} copy(bf16[1,4,1,64,256]{4,3,2,1,0:T(8,128)(2,1)S(1)} %bitcast.7) | data formatting | bytes 262144
  47.4 0.7 %copy.13 = bf16[8,64,256]{2,1,0:T(8,128)(2,1)} copy(bf16[8,64,256]{2,1,0:T(8,128)(2,1)S(1)} %get-tuple-element.9) | data formatting | bytes 524288

commit v4 on v3

--- a/solution.py
+++ b/solution.py
@@ -29,7 +29,7 @@
     S, R, C,
     pat, rhs_h, linv_h, coup_h, trhs_h, tinv_h, tf_h,
     out, top,
-    rhs, ginv, gt, coup, y, u, ub, d1, v, d2, tf, ti, tr, W, res, xf,
+    rhs, ginv, gt, coup, y, u, ub, d1, v, d2, tf, ti, tr, W, FW, res, xf,
     fws, fwr, xs, x, acc, cx, pf, px,
     ld, cp_sem, y_ss, y_rs, tf_ss, tf_rs, d1_ss, d1_rs, d2_ss, d2_rs,
     fw_ss, fw_rs, x1_ss, x1_rs, x2_ss, x2_rs, cx_ss, cx_rs, px_ss, px_rs,
@@ -229,9 +229,28 @@
     def lead_of(o):
         return (o * Kc) // Kr
 
-    def x2_copy(g, p):
+    def x2_copy(g, p, rr):
         place = x.at[pl.ds(g * Kc, Kc), mine]
-        return remote(place, place, x2_ss.at[g, p], x2_rs.at[g, p], (lax.rem(s + p, S), r, c))
+        return remote(
+            place, place, x2_ss.at[g, rr, p], x2_rs.at[g, p], (lax.rem(s + p, S), rr, c)
+        )
+
+    def x2_each(g, act):
+        @pl.when(r == lead_of(g))
+        def _():
+            for rr in range(R):
+                for p in range(S):
+                    if p > 0:
+                        act(x2_copy(g, p, rr))
+                    else:
+                        has = jnp.logical_or(rr == r, jnp.logical_and(rr == lead, c < g))
+
+                        @pl.when(jnp.logical_not(has))
+                        def _(rr=rr):
+                            act(x2_copy(g, 0, rr))
+
+    def x2_forward(g):
+        x2_each(g, lambda copy: copy.start())
 
     def x1_wait(g):
         place = x.at[pl.ds(g * Kc, Kc), mine]
@@ -245,6 +264,30 @@
             tf_wait(lead + q)
         for k in range(Kc):
             w_row(k)
+
+        def next_products():
+            def row(k, carry):
+                for b in range(Kc):
+                    t = None
+                    for m in range(b, Kc):
+                        term = dot_nn(tf[(c + 1) * Kc + k, m], W[blk(m), blk(b)])
+                        t = term if t is None else t + term
+                    FW[pl.ds(pl.multiple_of(k * B, B), B), blk(b)] = t.astype(BF)
+                return carry
+
+            lax.fori_loop(0, Kc, row, 0)
+
+        @pl.when(c > 0)
+        def _():
+            for rr in range(R):
+                @pl.when(rr >= lead + Q)
+                def _(rr=rr):
+                    tf_wait(rr)
+
+        @pl.when(jnp.logical_and(c > 0, c < C - 1))
+        def _():
+            next_products()
+
         tr_copy.wait()
         for q in range(Q):
             for o in range(C):
@@ -269,30 +312,54 @@
                 for k in range(Kc):
                     res[k] = res[k] - fwr[o, k].astype(F32)
         rb = [res[k].astype(BF) for k in range(Kc)]
-        fb = []
+
+        @pl.when(jnp.logical_and(c > 0, c < C - 1))
+        def _():
+            for k in range(Kc):
+                t = None
+                for b in range(Kc):
+                    term = dot_nt(rb[b], FW[blk(k), blk(b)])
+                    t = term if t is None else t + term
+                fws[c + 1, k] = t.astype(BF)
+            fw_copy(c, c + 1).start()
+
         for k in range(Kc):
             t = dot_nt(rb[k], W[blk(k), blk(k)])
             for b in range(k):
                 t = t + dot_nt(rb[b], W[blk(k), blk(b)])
-            fb.append(t.astype(BF))
-            xf[k] = fb[k]
-        for o in range(1, C):
-            @pl.when(c < o)
-            def _(o=o):
-                for rr in range(R):
-                    if (rr * Kr) // Kc == o:
-                        tf_wait(rr)
-                for k in range(Kc):
-                    t = None
-                    for b in range(Kc):
-                        term = dot_nt(xf[b], tf[o * Kc + k, b])
-                        t = term if t is None else t + term
-                    fws[o, k] = t.astype(BF)
-                fw_copy(c, o).start()
+            xf[k] = t.astype(BF)
+
+        def give(o):
+            for k in range(Kc):
+                t = None
+                for b in range(Kc):
+                    term = dot_nt(xf[b], tf[o * Kc + k, b])
+                    t = term if t is None else t + term
+                fws[o, k] = t.astype(BF)
+            fw_copy(c, o).start()
+
+        @pl.when(c == 0)
+        def _():
+            for rr in range(R):
+                if (rr * Kr) // Kc == 1:
+                    tf_wait(rr)
+            give(1)
+            for rr in range(R):
+                if (rr * Kr) // Kc > 1:
+                    tf_wait(rr)
+
+        for o in range(2, C):
+            @pl.when(c < o - 1)
+            def _(o=o):
+                give(o)
+
+        @pl.when(c == 0)
+        def _():
+            next_products()
         for k in range(Kc):
             res[k] = xf[k].astype(F32)
-        for o in range(C - 1, 0, -1):
-            @pl.when(c < o)
+        for o in range(C - 1, 1, -1):
+            @pl.when(c < o - 1)
             def _(o=o):
                 x1_wait(o)
                 for k in range(Kc):
@@ -300,35 +367,45 @@
                     for a in range(Kc):
                         t = t - dot_nn(x[o * Kc + a, mine, :], tf[o * Kc + a, k])
                     res[k] = t
-                for p in range(1, S):
-                    x2_copy(o, p).start()
+                x2_forward(o)
         wb = [res[k].astype(BF) for k in range(Kc)]
         for k in range(Kc):
             t = dot_nn(wb[k], W[blk(k), blk(k)])
             for a in range(k + 1, Kc):
                 t = t + dot_nn(wb[a], W[blk(a), blk(k)])
-            xs[k] = t.astype(BF)
+            res[k] = t
+
+        @pl.when(c < C - 1)
+        def _():
+            x1_wait(c + 1)
+            for k in range(Kc):
+                t = res[k]
+                for a in range(Kc):
+                    t = t - dot_nn(x[(c + 1) * Kc + a, mine, :], FW[blk(a), blk(k)])
+                res[k] = t
+        for k in range(Kc):
+            xs[k] = res[k].astype(BF)
         for o in range(C - 2, -1, -1):
             @pl.when(c > o)
             def _(o=o):
                 x1_copy(lead_of(o), o).start()
+        for o in range(C - 1, -1, -1):
+            @pl.when(jnp.logical_and(c != o, jnp.logical_or(c < o, lead_of(o) != lead)))
+            def _(o=o):
+                x1_copy(lead, o).start()
         for b in range(Kc):
             x[c * Kc + b, mine, :] = xs[b]
-        for p in range(1, S):
-            x2_copy(c, p).start()
-        for rr in range(R):
-            for o in range(C):
-                if rr != lead_of(o):
-                    x1_copy(rr, o).start()
-                else:
-                    @pl.when(c < o)
-                    def _(rr=rr, o=o):
-                        x1_copy(rr, o).start()
+        x2_forward(c)
+
+        @pl.when(c < C - 1)
+        def _():
+            x2_forward(c + 1)
 
     def x2_from(g, p):
         src = lax.rem(s + S - p, S)
+        row = lead_of(g)
         place = x.at[pl.ds(g * Kc, Kc), pl.ds(pl.multiple_of(src * ns, ns), ns)]
-        return remote(place, place, x2_ss.at[g, p], x2_rs.at[g, p], (src, r, c))
+        return remote(place, place, x2_ss.at[g, row, p], x2_rs.at[g, p], (src, row, c))
 
     cx_own.wait()
     for p in range(1, R):
@@ -337,11 +414,17 @@
         remote(pf.at[r], px.at[src], px_ss.at[p], px_rs.at[src], (s, src, c)).wait_recv()
 
     for g in range(C - 1, -1, -1):
-        @pl.when(jnp.logical_not(jnp.logical_and(is_lead, c <= g)))
+        late = jnp.logical_not(jnp.logical_and(is_lead, c <= g))
+
+        @pl.when(jnp.logical_and(late, r == lead_of(g)))
         def _():
             x1_wait(g)
-            for p in range(1, S):
-                x2_copy(g, p).start()
+            x2_forward(g)
+
+        @pl.when(jnp.logical_and(late, r != lead_of(g)))
+        def _():
+            x2_from(g, 0).wait_recv()
+
         for p in range(1, S):
             x2_from(g, p).wait_recv()
         for i in range(Ni):
@@ -374,8 +457,7 @@
             d2_send(j).wait_send()
 
     for g in range(C):
-        for p in range(1, S):
-            x2_copy(g, p).wait_send()
+        x2_each(g, lambda copy: copy.wait_send())
 
     @pl.when(is_lead)
     def _():
@@ -384,13 +466,13 @@
             def _(o=o):
                 fw_copy(c, o).wait_send()
 
-            for rr in range(R):
-                if rr != lead_of(o):
-                    x1_copy(rr, o).wait_send()
-                else:
-                    @pl.when(c != o)
-                    def _(rr=rr, o=o):
-                        x1_copy(rr, o).wait_send()
+            @pl.when(jnp.logical_and(c != o, c > o))
+            def _(o=o):
+                x1_copy(lead_of(o), o).wait_send()
+
+            @pl.when(jnp.logical_and(c != o, jnp.logical_or(c < o, lead_of(o) != lead)))
+            def _(o=o):
+                x1_copy(lead, o).wait_send()
 
 
 def local(sizes, leaf_rhs, leaf_inverse, coupling, pattern, top_rhs, top_inverse, top_factor):
@@ -410,14 +492,14 @@
         V((Kr, R, Ni, B, B), BF), V((R, Ni, n, B), BF),
         V((Kr, n, B), F32), V((Kr, n, B), BF), V((S, Kr, ns, B), BF), V((Kr, ns, B), BF),
         V((C, Kc, ns, B), BF), V((KT, Kc, B, B), BF), V((Kc, B, B), BF), V((Kc, ns, B), BF),
-        V((Kc * B, Kc * B), BF), V((Kc, ns, B), F32), V((Kc, ns, B), BF),
+        V((Kc * B, Kc * B), BF), V((Kc * B, Kc * B), BF), V((Kc, ns, B), F32), V((Kc, ns, B), BF),
         V((C, Kc, ns, B), BF), V((C, Kc, ns, B), BF), V((Kc, ns, B), BF),
         V((KT, n, B), BF), V((Ni, n, B), F32), V((R, Kr, Ni, B, B), BF),
         V((R, Kr, Ni, 8, B), F32), V((R, Kr, Ni, 8, B), F32),
         D((6,)), D((Kr, R)), D((R,)), D((R,)), D, D((R,)),
         D((chunks, S)), D((chunks, S)), D((chunks,)), D((Q, C)),
         D((C,)), D((C,)),
-        D((R, C)), D((C,)), D((C, S)), D((C, S)), D((R,)), D((R,)), D((R,)), D((R,)),
+        D((R, C)), D((C,)), D((C, R, S)), D((C, S)), D((R,)), D((R,)), D((R,)), D((R,)),
     ]
     leaf, top = pl.pallas_call(
         functools.partial(kernel, S, R, C),

time: 48.3 us -> 45.4 us (0.940)
  Pallas kernels: 46.1 us -> 43.2 us
    pallas_call x1, Pallas kernels: 46.1 us -> 43.2 us  [local(): pl.pallas_call(functools.partial(kernel, S, R, C), out_shape=(pltpu.VMEM(...]
where the time goes in v4:
time: 45.4 us; the launch traced here: 45.2 us
  Pallas kernels  43.2 us (95%)
  local copies, waits for them, and re-layouts  1.36 us (3%)
  between operations  0.64 us (1%)
    pallas_call x1, Pallas kernels, local(): pl.pallas_call(functools.partial(kernel, S, R, C), out_shape=(pltpu.VMEM(...  43.2 us
    unnamed x2, local copies, waits for them, and re-layouts  1.36 us

profile of v4, /device:TPU:1, one launch (start us, length us, event | category | flops | bytes accessed | tf_op | source)
XLA Modules:
  0.0 45.2 jit_solution(543985540664975065)
XLA Ops:
  0.6 43.2 %shard_map.86 = (bf16[4,64,256]{2,1,0:T(8,128)(2,1)S(1)}, bf16[8,64,256]{2,1,0:T(8,128)(2,1)S(1)}) custom-call(s32[8,8]{1,0:T(8,128)} %bitcast.11, bf16[4,64,256]{2,1,0:T(8,128)(2,1)} %bitcast.10, bf16[4,256,256]{2,1,0:T(8,128)(2,1)} %bitcast.9, bf16[8,2,4,256,256]{4,3,2,1,0:T(8,128)(2,1)} %bitcast.8, bf16[16,64,256]{2,1,0:T(8,128)(2,1)} %trhs_h.1, ...), custom_call_target="tpu_custom_call" | custom-call | tf_op jit(solution)/shard_map/pallas_call | solution.py:504
  43.8 0.7 %copy.12 = bf16[1,4,1,64,256]{4,3,2,1,0:T(8,128)(2,1)} copy(bf16[1,4,1,64,256]{4,3,2,1,0:T(8,128)(2,1)S(1)} %bitcast.7) | data formatting | bytes 262144
  44.5 0.7 %copy.13 = bf16[8,64,256]{2,1,0:T(8,128)(2,1)} copy(bf16[8,64,256]{2,1,0:T(8,128)(2,1)S(1)} %get-tuple-element.9) | data formatting | bytes 524288

commit v5 on v4

--- a/solution.py
+++ b/solution.py
@@ -66,19 +66,9 @@
         rr = lax.rem(r + p, R)
         return pltpu.make_async_copy(coup_h.at[a, rr], coup.at[a, rr], cp_sem.at[a, p])
 
-    for j in range(chunks):
-        for p in range(R):
-            for a in range(j * Kg, (j + 1) * Kg):
-                coup_copy(a, p).start()
     ti_copy = pltpu.make_async_copy(tinv_h.at[pl.ds(c * Kc, Kc)], ti, ld.at[2])
     tr_copy = pltpu.make_async_copy(trhs_h.at[pl.ds(c * Kc, Kc), mine], tr, ld.at[3])
     tf_copy = pltpu.make_async_copy(tf_h, tf.at[pl.ds(r * Kr, Kr)], ld.at[4])
-
-    @pl.when(is_lead)
-    def _():
-        ti_copy.start()
-        tr_copy.start()
-        tf_copy.start()
 
     barrier = pltpu.get_barrier_semaphore()
     for p in range(1, S):
@@ -94,8 +84,24 @@
                 device_id_type=pl.DeviceIdType.MESH,
             )
 
+    for rr in range(R):
+        for a in range(Kr):
+            for i in range(Ni):
+                pf[rr, a, i] = jnp.full((8, B), pat[a, rr * Ni + i].astype(F32))
+    px[r] = pf[r]
     for cp in loads:
         cp.wait()
+    for j in range(chunks):
+        for p in range(R):
+            for a in range(j * Kg, (j + 1) * Kg):
+                coup_copy(a, p).start()
+
+    @pl.when(is_lead)
+    def _():
+        ti_copy.start()
+        tr_copy.start()
+        tf_copy.start()
+
     for i in range(Ni):
         g = lower(ginv[i])
         gt[i] = g
@@ -164,6 +170,21 @@
     def self_lead(j):
         return jnp.logical_and(is_lead, group_of(j) == c)
 
+    def cx_send(p):
+        to = lax.rem(r + p, R)
+        return remote(coup_h.at[:, to], cx.at[r], cx_ss.at[p], cx_rs.at[r], (s, to, c))
+
+    def px_send(p):
+        to = lax.rem(r + p, R)
+        return remote(pf.at[to], px.at[r], px_ss.at[p], px_rs.at[r], (s, to, c))
+
+    cx_own = pltpu.make_async_copy(coup_h.at[:, r], cx.at[r], ld.at[5])
+    cx_own.start()
+    for p in range(1, R):
+        cx_send(p).start()
+    for p in range(1, R):
+        px_send(p).start()
+
     def blk(k):
         return pl.ds(k * B, B)
 
@@ -177,6 +198,18 @@
                 t = term if t is None else t + term
             W[blk(k), blk(b)] = (-dot_nn(g, t.astype(BF))).astype(BF)
 
+    def group_inverse():
+        ti_copy.wait()
+        tf_copy.wait()
+        for q in range(1, Q):
+            tf_wait(lead + q)
+        for k in range(Kc):
+            w_row(k)
+
+    @pl.when(jnp.logical_and(is_lead, c == 0))
+    def _():
+        group_inverse()
+
     for j in range(chunks):
         for p in range(1, S):
             d1_send(j, p).wait_recv()
@@ -195,26 +228,6 @@
         def _():
             d2_send(j).start()
 
-    def cx_send(p):
-        to = lax.rem(r + p, R)
-        return remote(coup_h.at[:, to], cx.at[r], cx_ss.at[p], cx_rs.at[r], (s, to, c))
-
-    def px_send(p):
-        to = lax.rem(r + p, R)
-        return remote(pf.at[to], px.at[r], px_ss.at[p], px_rs.at[r], (s, to, c))
-
-    cx_own = pltpu.make_async_copy(coup_h.at[:, r], cx.at[r], ld.at[5])
-    cx_own.start()
-    for p in range(1, R):
-        cx_send(p).start()
-    for rr in range(R):
-        for a in range(Kr):
-            for i in range(Ni):
-                pf[rr, a, i] = jnp.full((8, B), pat[a, rr * Ni + i].astype(F32))
-    px[r] = pf[r]
-    for p in range(1, R):
-        px_send(p).start()
-
     def fw_copy(src_c, dst_c):
         return remote(
             fws.at[dst_c], fwr.at[src_c], fw_ss.at[dst_c], fw_rs.at[src_c],
@@ -258,12 +271,9 @@
 
     @pl.when(is_lead)
     def _():
-        ti_copy.wait()
-        tf_copy.wait()
-        for q in range(1, Q):
-            tf_wait(lead + q)
-        for k in range(Kc):
-            w_row(k)
+        @pl.when(c > 0)
+        def _():
+            group_inverse()
 
         def next_products():
             def row(k, carry):

time: 45.4 us -> 45.8 us (level)
    pallas_call x1, Pallas kernels: 43.2 us -> 43.6 us  [local(): pl.pallas_call(functools.partial(kernel, S, R, C), out_shape=(pltpu.VMEM(...]
where the time goes in v5:
time: 45.8 us; the launch traced here: 45.6 us
  Pallas kernels  43.6 us (95%)
  local copies, waits for them, and re-layouts  1.36 us (3%)
  between operations  0.64 us (1%)
    pallas_call x1, Pallas kernels, local(): pl.pallas_call(functools.partial(kernel, S, R, C), out_shape=(pltpu.VMEM(...  43.6 us
    unnamed x2, local copies, waits for them, and re-layouts  1.36 us

profile of v5, /device:TPU:1, one launch (start us, length us, event | category | flops | bytes accessed | tf_op | source)
XLA Modules:
  0.0 45.6 jit_solution(11089957574025083509)
XLA Ops:
  0.6 43.6 %shard_map.86 = (bf16[4,64,256]{2,1,0:T(8,128)(2,1)S(1)}, bf16[8,64,256]{2,1,0:T(8,128)(2,1)S(1)}) custom-call(s32[8,8]{1,0:T(8,128)} %bitcast.11, bf16[4,64,256]{2,1,0:T(8,128)(2,1)} %bitcast.10, bf16[4,256,256]{2,1,0:T(8,128)(2,1)} %bitcast.9, bf16[8,2,4,256,256]{4,3,2,1,0:T(8,128)(2,1)} %bitcast.8, bf16[16,64,256]{2,1,0:T(8,128)(2,1)} %trhs_h.1, ...), custom_call_target="tpu_custom_call" | custom-call | tf_op jit(solution)/shard_map/pallas_call | solution.py:514
  44.3 0.7 %copy.12 = bf16[1,4,1,64,256]{4,3,2,1,0:T(8,128)(2,1)} copy(bf16[1,4,1,64,256]{4,3,2,1,0:T(8,128)(2,1)S(1)} %bitcast.7) | data formatting | bytes 262144
  44.9 0.7 %copy.13 = bf16[8,64,256]{2,1,0:T(8,128)(2,1)} copy(bf16[8,64,256]{2,1,0:T(8,128)(2,1)S(1)} %get-tuple-element.9) | data formatting | bytes 524288

commit v6 on v5

--- a/solution.py
+++ b/solution.py
@@ -170,21 +170,6 @@
     def self_lead(j):
         return jnp.logical_and(is_lead, group_of(j) == c)
 
-    def cx_send(p):
-        to = lax.rem(r + p, R)
-        return remote(coup_h.at[:, to], cx.at[r], cx_ss.at[p], cx_rs.at[r], (s, to, c))
-
-    def px_send(p):
-        to = lax.rem(r + p, R)
-        return remote(pf.at[to], px.at[r], px_ss.at[p], px_rs.at[r], (s, to, c))
-
-    cx_own = pltpu.make_async_copy(coup_h.at[:, r], cx.at[r], ld.at[5])
-    cx_own.start()
-    for p in range(1, R):
-        cx_send(p).start()
-    for p in range(1, R):
-        px_send(p).start()
-
     def blk(k):
         return pl.ds(k * B, B)
 
@@ -228,6 +213,21 @@
         def _():
             d2_send(j).start()
 
+    def cx_send(p):
+        to = lax.rem(r + p, R)
+        return remote(coup_h.at[:, to], cx.at[r], cx_ss.at[p], cx_rs.at[r], (s, to, c))
+
+    def px_send(p):
+        to = lax.rem(r + p, R)
+        return remote(pf.at[to], px.at[r], px_ss.at[p], px_rs.at[r], (s, to, c))
+
+    cx_own = pltpu.make_async_copy(coup_h.at[:, r], cx.at[r], ld.at[5])
+    cx_own.start()
+    for p in range(1, R):
+        cx_send(p).start()
+    for p in range(1, R):
+        px_send(p).start()
+
     def fw_copy(src_c, dst_c):
         return remote(
             fws.at[dst_c], fwr.at[src_c], fw_ss.at[dst_c], fw_rs.at[src_c],
@@ -287,14 +287,14 @@
 
             lax.fori_loop(0, Kc, row, 0)
 
-        @pl.when(c > 0)
+        @pl.when(c > 1)
         def _():
             for rr in range(R):
                 @pl.when(rr >= lead + Q)
                 def _(rr=rr):
                     tf_wait(rr)
 
-        @pl.when(jnp.logical_and(c > 0, c < C - 1))
+        @pl.when(jnp.logical_and(c > 1, c < C - 1))
         def _():
             next_products()
 
@@ -323,7 +323,7 @@
                     res[k] = res[k] - fwr[o, k].astype(F32)
         rb = [res[k].astype(BF) for k in range(Kc)]
 
-        @pl.when(jnp.logical_and(c > 0, c < C - 1))
+        @pl.when(jnp.logical_and(c > 1, c < C - 1))
         def _():
             for k in range(Kc):
                 t = None
@@ -348,22 +348,23 @@
                 fws[o, k] = t.astype(BF)
             fw_copy(c, o).start()
 
-        @pl.when(c == 0)
-        def _():
-            for rr in range(R):
-                if (rr * Kr) // Kc == 1:
-                    tf_wait(rr)
-            give(1)
-            for rr in range(R):
-                if (rr * Kr) // Kc > 1:
-                    tf_wait(rr)
+        for first in range(2):
+            @pl.when(c == first)
+            def _(first=first):
+                for rr in range(R):
+                    if (rr * Kr) // Kc == first + 1:
+                        tf_wait(rr)
+                give(first + 1)
+                for rr in range(R):
+                    if (rr * Kr) // Kc > first + 1:
+                        tf_wait(rr)
 
         for o in range(2, C):
             @pl.when(c < o - 1)
             def _(o=o):
                 give(o)
 
-        @pl.when(c == 0)
+        @pl.when(c <= 1)
         def _():
             next_products()
         for k in range(Kc):

time: 45.8 us -> 46.3 us (1.011)
  Pallas kernels: 43.6 us -> 44.1 us
where the time goes in v6:
time: 46.3 us; the launch traced here: 46.1 us
  Pallas kernels  44.1 us (95%)
  local copies, waits for them, and re-layouts  1.36 us (3%)
  between operations  0.64 us (1%)
    pallas_call x1, Pallas kernels, local(): pl.pallas_call(functools.partial(kernel, S, R, C), out_shape=(pltpu.VMEM(...  44.1 us
    unnamed x2, local copies, waits for them, and re-layouts  1.36 us

profile of v6, /device:TPU:1, one launch (start us, length us, event | category | flops | bytes accessed | tf_op | source)
XLA Modules:
  0.0 46.1 jit_solution(3396267192877688395)
XLA Ops:
  0.6 44.1 %shard_map.86 = (bf16[4,64,256]{2,1,0:T(8,128)(2,1)S(1)}, bf16[8,64,256]{2,1,0:T(8,128)(2,1)S(1)}) custom-call(s32[8,8]{1,0:T(8,128)} %bitcast.11, bf16[4,64,256]{2,1,0:T(8,128)(2,1)} %bitcast.10, bf16[4,256,256]{2,1,0:T(8,128)(2,1)} %bitcast.9, bf16[8,2,4,256,256]{4,3,2,1,0:T(8,128)(2,1)} %bitcast.8, bf16[16,64,256]{2,1,0:T(8,128)(2,1)} %trhs_h.1, ...), custom_call_target="tpu_custom_call" | custom-call | tf_op jit(solution)/shard_map/pallas_call | solution.py:515
  44.7 0.7 %copy.12 = bf16[1,4,1,64,256]{4,3,2,1,0:T(8,128)(2,1)} copy(bf16[1,4,1,64,256]{4,3,2,1,0:T(8,128)(2,1)S(1)} %bitcast.7) | data formatting | bytes 262144
  45.4 0.7 %copy.13 = bf16[8,64,256]{2,1,0:T(8,128)(2,1)} copy(bf16[8,64,256]{2,1,0:T(8,128)(2,1)S(1)} %get-tuple-element.9) | data formatting | bytes 524288

commit v7 on v4

--- a/solution.py
+++ b/solution.py
@@ -138,6 +138,48 @@
             ub.at[blocks, rows], d1.at[p, blocks], d1_ss.at[j, p], d1_rs.at[j, p], (to, r, c)
         )
 
+    def d2_send(j):
+        g = group_of(j)
+        pos = lax.rem(r * Kr + j * Kg, Kc)
+        return remote(
+            v.at[pl.ds(j * Kg, Kg)], d2.at[c, pl.ds(pos, Kg)], d2_ss.at[j],
+            d2_rs.at[pos // Kg, c], (s, (g * Kc) // Kr, g),
+        )
+
+    def self_lead(j):
+        return jnp.logical_and(is_lead, group_of(j) == c)
+
+    def blk(k):
+        return pl.ds(k * B, B)
+
+    def w_row(k):
+        g = lower(ti[k])
+        W[blk(k), blk(k)] = g
+        for b in range(k):
+            t = None
+            for m in range(b, k):
+                term = dot_nn(tf[c * Kc + k, m], W[blk(m), blk(b)])
+                t = term if t is None else t + term
+            W[blk(k), blk(b)] = (-dot_nn(g, t.astype(BF))).astype(BF)
+
+    def pass_on(j):
+        for p in range(1, S):
+            d1_send(j, p).wait_recv()
+        for b in range(Kg):
+            a = j * Kg + b
+            total = u[a, mine, :]
+            for p in range(1, S):
+                total = total + d1[p, a].astype(F32)
+            v[a] = total.astype(BF)
+
+        @pl.when(self_lead(j))
+        def _():
+            d2[c, pl.ds(0, Kg)] = v[pl.ds(j * Kg, Kg)]
+
+        @pl.when(jnp.logical_not(self_lead(j)))
+        def _():
+            d2_send(j).start()
+
     for j in range(chunks):
         blocks = range(j * Kg, (j + 1) * Kg)
         for p in range(R):
@@ -150,50 +192,11 @@
                 u[a] = total
                 if p == R - 1:
                     ub[a] = total.astype(BF)
+            if j > 0 and p == 0:
+                pass_on(j - 1)
         for t in range(1, S):
             d1_send(j, t).start()
-
-    def d2_send(j):
-        g = group_of(j)
-        pos = lax.rem(r * Kr + j * Kg, Kc)
-        return remote(
-            v.at[pl.ds(j * Kg, Kg)], d2.at[c, pl.ds(pos, Kg)], d2_ss.at[j],
-            d2_rs.at[pos // Kg, c], (s, (g * Kc) // Kr, g),
-        )
-
-    def self_lead(j):
-        return jnp.logical_and(is_lead, group_of(j) == c)
-
-    def blk(k):
-        return pl.ds(k * B, B)
-
-    def w_row(k):
-        g = lower(ti[k])
-        W[blk(k), blk(k)] = g
-        for b in range(k):
-            t = None
-            for m in range(b, k):
-                term = dot_nn(tf[c * Kc + k, m], W[blk(m), blk(b)])
-                t = term if t is None else t + term
-            W[blk(k), blk(b)] = (-dot_nn(g, t.astype(BF))).astype(BF)
-
-    for j in range(chunks):
-        for p in range(1, S):
-            d1_send(j, p).wait_recv()
-        for b in range(Kg):
-            a = j * Kg + b
-            total = u[a, mine, :]
-            for p in range(1, S):
-                total = total + d1[p, a].astype(F32)
-            v[a] = total.astype(BF)
-
-        @pl.when(self_lead(j))
-        def _():
-            d2[c, pl.ds(0, Kg)] = v[pl.ds(j * Kg, Kg)]
-
-        @pl.when(jnp.logical_not(self_lead(j)))
-        def _():
-            d2_send(j).start()
+    pass_on(chunks - 1)
 
     def cx_send(p):
         to = lax.rem(r + p, R)

time: 45.4 us -> 48 us (1.057)
  Pallas kernels: 43.2 us -> 45.8 us
    pallas_call x1, Pallas kernels: 43.2 us -> 45.8 us  [local(): pl.pallas_call(functools.partial(kernel, S, R, C), out_shape=(pltpu.VMEM(...]
where the time goes in v7:
time: 48 us; the launch traced here: 47.8 us
  Pallas kernels  45.8 us (95%)
  local copies, waits for them, and re-layouts  1.36 us (3%)
  between operations  0.64 us (1%)
    pallas_call x1, Pallas kernels, local(): pl.pallas_call(functools.partial(kernel, S, R, C), out_shape=(pltpu.VMEM(...  45.8 us
    unnamed x2, local copies, waits for them, and re-layouts  1.36 us

profile of v7, /device:TPU:1, one launch (start us, length us, event | category | flops | bytes accessed | tf_op | source)
XLA Modules:
  0.0 47.8 jit_solution(6294029817653432870)
XLA Ops:
  0.6 45.8 %shard_map.86 = (bf16[4,64,256]{2,1,0:T(8,128)(2,1)S(1)}, bf16[8,64,256]{2,1,0:T(8,128)(2,1)S(1)}) custom-call(s32[8,8]{1,0:T(8,128)} %bitcast.11, bf16[4,64,256]{2,1,0:T(8,128)(2,1)} %bitcast.10, bf16[4,256,256]{2,1,0:T(8,128)(2,1)} %bitcast.9, bf16[8,2,4,256,256]{4,3,2,1,0:T(8,128)(2,1)} %bitcast.8, bf16[16,64,256]{2,1,0:T(8,128)(2,1)} %trhs_h.1, ...), custom_call_target="tpu_custom_call" | custom-call | tf_op jit(solution)/shard_map/pallas_call | solution.py:507
  46.4 0.7 %copy.12 = bf16[1,4,1,64,256]{4,3,2,1,0:T(8,128)(2,1)} copy(bf16[1,4,1,64,256]{4,3,2,1,0:T(8,128)(2,1)S(1)} %bitcast.7) | data formatting | bytes 262144
  47.1 0.7 %copy.13 = bf16[8,64,256]{2,1,0:T(8,128)(2,1)} copy(bf16[8,64,256]{2,1,0:T(8,128)(2,1)S(1)} %get-tuple-element.9) | data formatting | bytes 524288
